TPU v7x, 32 devices: a whole 2x2x4 slice. The times are simulated.
32 devices in a mesh: sweep: 4 (over z), lat: 8 (over y, x, core).
Axes of the slice: x: 2, y: 2, z: 4, core: 2. Of those that a mesh axis runs over, the one named last changes fastest.
Arguments:
- traveltime: float32 [2, 32, 128, 384], P(None, 'sweep', 'lat'), may hold values from 0 to 4
- residual: float32 [2, 32, 128, 384], P(None, 'sweep', 'lat'), may hold values from -6 to 6
- slowness: float32 [32, 128, 384], P('sweep', 'lat'), may hold values from 0.3 to 0.6
- attenuation: float32 [32, 128, 384], P('sweep', 'lat'), may hold values from 0.005 to 0.05
- topography: int32 [128, 384], P('lat'), may hold values from 0 to 31, as said below
Outputs:
- adjoint: float32 [2, 32, 128, 384], P(None, 'sweep', 'lat')
- gradient: float32 [32, 128, 384], P('sweep', 'lat')
Inputs may be any that keep to these rules, and one draw needn't show every extreme that they name: Apart from two corner columns, topography is a level shared by each aligned strip of 16 columns along the first lateral dimension plus a small rough offset per column, so that whole blocks of planes lie above it; the first column of the grid has topography 32 - 1 and the last column 0.
All inputs are finite; a program needn't handle non-finite values.
Results may differ from a plain program's by a relative error of at most 0.0003.
Values sent between devices are 32-bit elements; how exact they have to be, the bound alone decides.
A program may use at most 64 MiB of HBM per device.

v0:
```python
import jax
import jax.numpy as jnp
from jax import lax
from jax.sharding import PartitionSpec as P


def extended(cells, sides, width):
    for axis, dim in sides:
        count = lax.axis_size(axis)
        ends = count - 1
        head = lax.slice_in_dim(cells, 0, width, axis=dim)
        tail = lax.slice_in_dim(cells, cells.shape[dim] - width, cells.shape[dim], axis=dim)
        cells = jnp.concatenate(
            [
                lax.ppermute(tail, axis, [(i, (i + 1) % count) for i in range(ends)]),
                cells,
                lax.ppermute(head, axis, [((i + 1) % count, i) for i in range(ends)]),
            ],
            axis=dim,
        )
    return cells


def shifted(block, axis, distance):
    devices = range(lax.axis_size(axis))
    route = [(i - distance, i) for i in devices if i - distance in devices]
    return lax.ppermute(block, axis, route)


def shift_low(field, along):
    count = field.shape[along]
    padding = jnp.zeros_like(lax.slice_in_dim(field, 0, 1, axis=along))
    return jnp.concatenate([padding, lax.slice_in_dim(field, 0, count - 1, axis=along)], axis=along)


def shift_high(field, along):
    count = field.shape[along]
    padding = jnp.zeros_like(lax.slice_in_dim(field, 0, 1, axis=along))
    return jnp.concatenate([lax.slice_in_dim(field, 1, count, axis=along), padding], axis=along)


def upwind_weights(tau_wide):
    last = tau_wide.ndim - 1
    center = tau_wide[..., 1:-1, :]
    west = jax.nn.softplus(center - tau_wide[..., :-2, :])
    east = jax.nn.softplus(center - tau_wide[..., 2:, :])
    north = jax.nn.softplus(center - shift_low(center, last))
    south = jax.nn.softplus(center - shift_high(center, last))
    return (west, east, north, south)


def shards(traveltime, residual, slowness, attenuation, topography):
    sources, planes, columns, crosses = traveltime.shape
    plane_index = lax.axis_index("sweep") * planes + lax.iota(jnp.int32, planes)
    active = (plane_index[:, None, None] >= topography[None]).astype(jnp.float32)
    packed = jnp.concatenate(
        [traveltime, residual, slowness[None], attenuation[None], active[None]], axis=0
    )
    inputs_wide = extended(packed, (("lat", 2),), planes + 1)
    west, east, north, south = upwind_weights(inputs_wide[:sources])
    source_wide = inputs_wide[sources : 2 * sources, :, 1:-1]
    slow_wide = inputs_wide[2 * sources, :, 1:-1]
    atten_wide = inputs_wide[2 * sources + 1, :, 1:-1]
    active_wide = inputs_wide[2 * sources + 2, :, 1:-1]
    denominator = slow_wide + west + east + north + south + atten_wide
    scale = active_wide / denominator
    widened = jnp.concatenate(
        [source_wide, west, east, north, south, scale, slow_wide[None]], axis=0
    )
    source_w = widened[0:sources]
    west_w = widened[sources : 2 * sources]
    east_w = widened[2 * sources : 3 * sources]
    north_w = widened[3 * sources : 4 * sources]
    south_w = widened[4 * sources : 5 * sources]
    scale_w = widened[5 * sources : 6 * sources]
    slow_w = widened[6 * sources]

    def update_block(previous):
        results = []
        for level in range(planes):
            current = scale_w[:, level] * (
                source_w[:, level]
                + slow_w[level] * previous
                + west_w[:, level] * shift_low(previous, 1)
                + east_w[:, level] * shift_high(previous, 1)
                + north_w[:, level] * shift_low(previous, 2)
                + south_w[:, level] * shift_high(previous, 2)
            )
            results.append(current[:, planes : planes + columns])
            previous = current
        return jnp.stack(results, axis=1)

    def advance(counter, carried):
        inflow, current_block = carried
        previous = extended(inflow, (("lat", 1),), planes)
        new_block = update_block(previous)
        new_inflow = shifted(new_block[:, -1], "sweep", 1)
        return (new_inflow, new_block)

    start = (
        jnp.zeros((sources, columns, crosses), jnp.float32),
        jnp.zeros((sources, planes, columns, crosses), jnp.float32),
    )
    _, adjoint = lax.fori_loop(0, lax.axis_size("sweep"), advance, start)
    gradient = slowness * jnp.sum(adjoint, axis=0)
    return (adjoint, gradient)


def solution(mesh):
    in_specs = (
        P(None, "sweep", "lat", None),
        P(None, "sweep", "lat", None),
        P("sweep", "lat", None),
        P("sweep", "lat", None),
        P("lat", None),
    )
    out_specs = (P(None, "sweep", "lat", None), P("sweep", "lat", None))
    return jax.shard_map(shards, mesh=mesh, in_specs=in_specs, out_specs=out_specs, check_vma=False)
```

profile of v0, /device:TPU:12, one launch (start us, length us, event | category | flops | bytes accessed | tf_op | source)
XLA Modules:
  0.0 139.8 jit_solution(9788182047366834385)
XLA Ops:
  4.2 1.9 %collective-permute-start.3 = (f32[7,8,9,384]{3,1,2,0:T(8,128)}, f32[7,8,9,384]{3,1,2,0:T(8,128)S(1)}, u32[]{:S(2)}, u32[]{:S(2)}) collective-permute-start(f32[7,8,9,384]{3,1,2,0:T(8,128)} %get-tuple-element.151), channel_id=1, source_target_pairs={{0,1},{1,2},{2,3},{3,4},{4,5},{5,6},{6,7},{8,9},{9,10},{10,11},{11... | collective-permute-start | bytes 2322440 | tf_op jit(solution)/shard_map/ppermute | solution.py:15
  6.1 4.5 %collective-permute-start.4 = (f32[7,8,9,384]{3,1,2,0:T(8,128)S(1)}, f32[7,8,9,384]{3,1,2,0:T(8,128)}, u32[]{:S(2)}, u32[]{:S(2)}) collective-permute-start(f32[7,8,9,384]{3,1,2,0:T(8,128)S(1)} %get-tuple-element.152), channel_id=1, source_target_pairs={{1,0},{2,1},{3,2},{4,3},{5,4},{6,5},{7,6},{9,8},{10,9},{11,10},{12... | collective-permute-start | bytes 2322440 | tf_op jit(solution)/shard_map/ppermute | solution.py:17
  10.7 13.5 %collective-permute-done.3 = f32[7,8,9,384]{3,1,2,0:T(8,128)S(1)} collective-permute-done((f32[7,8,9,384]{3,1,2,0:T(8,128)}, f32[7,8,9,384]{3,1,2,0:T(8,128)S(1)}, u32[]{:S(2)}, u32[]{:S(2)}) %collective-permute-start.3) | collective-permute-done | bytes 774176 | tf_op jit(solution)/shard_map/ppermute | solution.py:15
  24.9 1.3 pad_maximum_fusion
  26.7 2.0 %add_divide_fusion = (f32[2,8,32,384]{3,1,2,0:T(8,128)S(1)}, f32[2,8,32,384]{3,1,2,0:T(8,128)S(1)}, f32[2,8,32,384]{3,1,2,0:T(8,128)S(1)}, f32[2,8,32,384]{3,1,2...) fusion(f32[8,32,384]{2,0,1:T(8,128)S(1)} %get-tuple-element.149, ...), kind=kLoop, calls=%fused_computation.120 | loop fusion | flops 6684672 | bytes 10612736 | tf_op jit(solution)/shard_map/div | solution.py:66
  34.9 101.4 %while.12 = (s32[]{:T(128)}, f32[2,16,384]{2,1,0:T(8,128)S(1)}, f32[2,8,16,384]{3,2,0,1:T(8,128)}, f32[2,8,32,384]{3,2,0,1:T(8,128)}, f32[2,8,32,384]{3,2,0,1:T(...) while((s32[]{:T(128)}, f32[2,16,384]{2,1,0:T(8,128)S(1)}, ...), condition=%wide.region_1.2_spmd, body=%wide.region_0.1_spmd.sunk | while | flops 2039810 | bytes 20638464 | solution.py:104
  34.9 1.9 %collective-permute-start = (f32[2,8,384]{2,1,0:T(8,128)S(1)}, f32[2,8,384]{2,1,0:T(8,128)S(1)}, u32[]{:S(2)}, u32[]{:S(2)}) collective-permute-start(f32[2,8,384]{2,1,0:T(8,128)S(1)} %get-tuple-element.264), channel_id=1, source_target_pairs={{0,1},{1,2},{2,3},{3,4},{4,5},{5,6},{6,7},{8,9},{9,10},{10,11},{11... | collective-permute-start | bytes 73736 | tf_op jit(solution)/shard_map/while/body/eval_jaxpr/ppermute | solution.py:15
  36.8 4.8 %collective-permute-start.1 = (f32[2,8,384]{2,1,0:T(8,128)S(1)}, f32[2,8,384]{2,1,0:T(8,128)S(1)}, u32[]{:S(2)}, u32[]{:S(2)}) collective-permute-start(f32[2,8,384]{2,1,0:T(8,128)S(1)} %get-tuple-element.265), channel_id=1, source_target_pairs={{1,0},{2,1},{3,2},{4,3},{5,4},{6,5},{7,6},{9,8},{10,9},{11,10},{12... | collective-permute-start | bytes 73736 | tf_op jit(solution)/shard_map/while/body/eval_jaxpr/ppermute | solution.py:17
  46.1 1.2 fusion.103
  47.5 1.2 fusion.107
  48.8 1.2 fusion.111
  50.2 1.2 fusion.115
  51.6 1.2 fusion.119
  52.9 1.2 broadcast_multiply_fusion.2
  54.5 3.5 %collective-permute-start.2 = (f32[2,16,384]{2,1,0:T(8,128)S(1)}, f32[2,16,384]{2,1,0:T(8,128)S(1)}, u32[]{:S(2)}, u32[]{:S(2)}) collective-permute-start(f32[2,16,384]{2,1,0:T(8,128)S(1)} %get-tuple-element.314), channel_id=1, source_target_pairs={{0,8},{8,16},{16,24},{1,9},{9,17},{17,25},{2,10},{10,18},{18,26},{... | collective-permute-start | bytes 147464 | tf_op jit(solution)/shard_map/while/body/eval_jaxpr/ppermute | solution.py:27
  58.0 2.5 %collective-permute-done.2 = f32[2,16,384]{2,1,0:T(8,128)S(1)} collective-permute-done((f32[2,16,384]{2,1,0:T(8,128)S(1)}, f32[2,16,384]{2,1,0:T(8,128)S(1)}, u32[]{:S(2)}, u32[]{:S(2)}) %collective-permute-start.2) | collective-permute-done | bytes 49184 | tf_op jit(solution)/shard_map/while/body/eval_jaxpr/ppermute | solution.py:27
  60.5 1.9 %collective-permute-start = (f32[2,8,384]{2,1,0:T(8,128)S(1)}, f32[2,8,384]{2,1,0:T(8,128)S(1)}, u32[]{:S(2)}, u32[]{:S(2)}) collective-permute-start(f32[2,8,384]{2,1,0:T(8,128)S(1)} %get-tuple-element.264), channel_id=1, source_target_pairs={{0,1},{1,2},{2,3},{3,4},{4,5},{5,6},{6,7},{8,9},{9,10},{10,11},{11... | collective-permute-start | bytes 73736 | tf_op jit(solution)/shard_map/while/body/eval_jaxpr/ppermute | solution.py:15
  62.4 4.5 %collective-permute-start.1 = (f32[2,8,384]{2,1,0:T(8,128)S(1)}, f32[2,8,384]{2,1,0:T(8,128)S(1)}, u32[]{:S(2)}, u32[]{:S(2)}) collective-permute-start(f32[2,8,384]{2,1,0:T(8,128)S(1)} %get-tuple-element.265), channel_id=1, source_target_pairs={{1,0},{2,1},{3,2},{4,3},{5,4},{6,5},{7,6},{9,8},{10,9},{11,10},{12... | collective-permute-start | bytes 73736 | tf_op jit(solution)/shard_map/while/body/eval_jaxpr/ppermute | solution.py:17
  70.0 1.2 fusion.99
  71.4 1.2 fusion.103
  72.8 1.2 fusion.107
  74.1 1.2 fusion.111
  75.5 1.2 fusion.115
  76.8 1.2 fusion.119
  78.2 1.2 broadcast_multiply_fusion.2
  79.8 3.5 %collective-permute-start.2 = (f32[2,16,384]{2,1,0:T(8,128)S(1)}, f32[2,16,384]{2,1,0:T(8,128)S(1)}, u32[]{:S(2)}, u32[]{:S(2)}) collective-permute-start(f32[2,16,384]{2,1,0:T(8,128)S(1)} %get-tuple-element.314), channel_id=1, source_target_pairs={{0,8},{8,16},{16,24},{1,9},{9,17},{17,25},{2,10},{10,18},{18,26},{... | collective-permute-start | bytes 147464 | tf_op jit(solution)/shard_map/while/body/eval_jaxpr/ppermute | solution.py:27
  83.3 2.5 %collective-permute-done.2 = f32[2,16,384]{2,1,0:T(8,128)S(1)} collective-permute-done((f32[2,16,384]{2,1,0:T(8,128)S(1)}, f32[2,16,384]{2,1,0:T(8,128)S(1)}, u32[]{:S(2)}, u32[]{:S(2)}) %collective-permute-start.2) | collective-permute-done | bytes 49184 | tf_op jit(solution)/shard_map/while/body/eval_jaxpr/ppermute | solution.py:27
  85.8 1.9 %collective-permute-start = (f32[2,8,384]{2,1,0:T(8,128)S(1)}, f32[2,8,384]{2,1,0:T(8,128)S(1)}, u32[]{:S(2)}, u32[]{:S(2)}) collective-permute-start(f32[2,8,384]{2,1,0:T(8,128)S(1)} %get-tuple-element.264), channel_id=1, source_target_pairs={{0,1},{1,2},{2,3},{3,4},{4,5},{5,6},{6,7},{8,9},{9,10},{10,11},{11... | collective-permute-start | bytes 73736 | tf_op jit(solution)/shard_map/while/body/eval_jaxpr/ppermute | solution.py:15
  87.7 4.5 %collective-permute-start.1 = (f32[2,8,384]{2,1,0:T(8,128)S(1)}, f32[2,8,384]{2,1,0:T(8,128)S(1)}, u32[]{:S(2)}, u32[]{:S(2)}) collective-permute-start(f32[2,8,384]{2,1,0:T(8,128)S(1)} %get-tuple-element.265), channel_id=1, source_target_pairs={{1,0},{2,1},{3,2},{4,3},{5,4},{6,5},{7,6},{9,8},{10,9},{11,10},{12... | collective-permute-start | bytes 73736 | tf_op jit(solution)/shard_map/while/body/eval_jaxpr/ppermute | solution.py:17
  96.7 1.2 fusion.103
  98.0 1.2 fusion.107
  99.4 1.2 fusion.111
  100.8 1.2 fusion.115
  102.1 1.2 fusion.119
  103.5 1.2 broadcast_multiply_fusion.2
  105.0 3.5 %collective-permute-start.2 = (f32[2,16,384]{2,1,0:T(8,128)S(1)}, f32[2,16,384]{2,1,0:T(8,128)S(1)}, u32[]{:S(2)}, u32[]{:S(2)}) collective-permute-start(f32[2,16,384]{2,1,0:T(8,128)S(1)} %get-tuple-element.314), channel_id=1, source_target_pairs={{0,8},{8,16},{16,24},{1,9},{9,17},{17,25},{2,10},{10,18},{18,26},{... | collective-permute-start | bytes 147464 | tf_op jit(solution)/shard_map/while/body/eval_jaxpr/ppermute | solution.py:27
  108.5 2.5 %collective-permute-done.2 = f32[2,16,384]{2,1,0:T(8,128)S(1)} collective-permute-done((f32[2,16,384]{2,1,0:T(8,128)S(1)}, f32[2,16,384]{2,1,0:T(8,128)S(1)}, u32[]{:S(2)}, u32[]{:S(2)}) %collective-permute-start.2) | collective-permute-done | bytes 49184 | tf_op jit(solution)/shard_map/while/body/eval_jaxpr/ppermute | solution.py:27
  111.0 1.9 %collective-permute-start = (f32[2,8,384]{2,1,0:T(8,128)S(1)}, f32[2,8,384]{2,1,0:T(8,128)S(1)}, u32[]{:S(2)}, u32[]{:S(2)}) collective-permute-start(f32[2,8,384]{2,1,0:T(8,128)S(1)} %get-tuple-element.264), channel_id=1, source_target_pairs={{0,1},{1,2},{2,3},{3,4},{4,5},{5,6},{6,7},{8,9},{9,10},{10,11},{11... | collective-permute-start | bytes 73736 | tf_op jit(solution)/shard_map/while/body/eval_jaxpr/ppermute | solution.py:15
  113.0 4.5 %collective-permute-start.1 = (f32[2,8,384]{2,1,0:T(8,128)S(1)}, f32[2,8,384]{2,1,0:T(8,128)S(1)}, u32[]{:S(2)}, u32[]{:S(2)}) collective-permute-start(f32[2,8,384]{2,1,0:T(8,128)S(1)} %get-tuple-element.265), channel_id=1, source_target_pairs={{1,0},{2,1},{3,2},{4,3},{5,4},{6,5},{7,6},{9,8},{10,9},{11,10},{12... | collective-permute-start | bytes 73736 | tf_op jit(solution)/shard_map/while/body/eval_jaxpr/ppermute | solution.py:17
  122.0 1.2 fusion.103
  123.3 1.2 fusion.107
  124.7 1.2 fusion.111
  126.0 1.2 fusion.115
  127.4 1.2 fusion.119
  128.8 1.2 broadcast_multiply_fusion.2
  130.3 3.5 %collective-permute-start.2 = (f32[2,16,384]{2,1,0:T(8,128)S(1)}, f32[2,16,384]{2,1,0:T(8,128)S(1)}, u32[]{:S(2)}, u32[]{:S(2)}) collective-permute-start(f32[2,16,384]{2,1,0:T(8,128)S(1)} %get-tuple-element.314), channel_id=1, source_target_pairs={{0,8},{8,16},{16,24},{1,9},{9,17},{17,25},{2,10},{10,18},{18,26},{... | collective-permute-start | bytes 147464 | tf_op jit(solution)/shard_map/while/body/eval_jaxpr/ppermute | solution.py:27
  133.8 2.5 %collective-permute-done.2 = f32[2,16,384]{2,1,0:T(8,128)S(1)} collective-permute-done((f32[2,16,384]{2,1,0:T(8,128)S(1)}, f32[2,16,384]{2,1,0:T(8,128)S(1)}, u32[]{:S(2)}, u32[]{:S(2)}) %collective-permute-start.2) | collective-permute-done | bytes 49184 | tf_op jit(solution)/shard_map/while/body/eval_jaxpr/ppermute | solution.py:27
  136.3 1.8 %copy.21 = f32[2,8,16,384]{3,2,1,0:T(8,128)} copy(f32[2,8,16,384]{3,2,0,1:T(8,128)} %get-tuple-element.66) | data formatting | bytes 786432
  (174 shorter events, 31.8 us)
Async XLA Ops:
  0.6 2.3 %copy-start.1 = (f32[8,16,384]{2,1,0:T(8,128)S(1)}, f32[8,16,384]{2,1,0:T(8,128)}, u32[]{:S(2)}) copy-start(f32[8,16,384]{2,1,0:T(8,128)} %param.9) | copy-start | bytes 589828
  0.6 2.4 %copy-start.2 = (f32[8,16,384]{2,1,0:T(8,128)S(1)}, f32[8,16,384]{2,1,0:T(8,128)}, u32[]{:S(2)}) copy-start(f32[8,16,384]{2,1,0:T(8,128)} %param.10) | copy-start | bytes 589828
  0.7 2.5 %copy-start.3 = (s32[16,384]{1,0:T(8,128)S(1)}, s32[16,384]{1,0:T(8,128)}, u32[]{:S(2)}) copy-start(s32[16,384]{1,0:T(8,128)} %param.11) | copy-start | bytes 73732
  4.2 20.0 %collective-permute-start.3 = (f32[7,8,9,384]{3,1,2,0:T(8,128)}, f32[7,8,9,384]{3,1,2,0:T(8,128)S(1)}, u32[]{:S(2)}, u32[]{:S(2)}) collective-permute-start(f32[7,8,9,384]{3,1,2,0:T(8,128)} %get-tuple-element.151), channel_id=1, source_target_pairs={{0,1},{1,2},{2,3},{3,4},{4,5},{5,6},{6,7},{8,9},{9,10},{10,11},{11... | collective-permute-start | bytes 2322440 | tf_op jit(solution)/shard_map/ppermute | solution.py:15
  6.1 18.8 %collective-permute-start.4 = (f32[7,8,9,384]{3,1,2,0:T(8,128)S(1)}, f32[7,8,9,384]{3,1,2,0:T(8,128)}, u32[]{:S(2)}, u32[]{:S(2)}) collective-permute-start(f32[7,8,9,384]{3,1,2,0:T(8,128)S(1)} %get-tuple-element.152), channel_id=1, source_target_pairs={{1,0},{2,1},{3,2},{4,3},{5,4},{6,5},{7,6},{9,8},{10,9},{11,10},{12... | collective-permute-start | bytes 2322440 | tf_op jit(solution)/shard_map/ppermute | solution.py:17
  34.9 9.7 %collective-permute-start = (f32[2,8,384]{2,1,0:T(8,128)S(1)}, f32[2,8,384]{2,1,0:T(8,128)S(1)}, u32[]{:S(2)}, u32[]{:S(2)}) collective-permute-start(f32[2,8,384]{2,1,0:T(8,128)S(1)} %get-tuple-element.264), channel_id=1, source_target_pairs={{0,1},{1,2},{2,3},{3,4},{4,5},{5,6},{6,7},{8,9},{9,10},{10,11},{11... | collective-permute-start | bytes 73736 | tf_op jit(solution)/shard_map/while/body/eval_jaxpr/ppermute | solution.py:15
  36.8 7.8 %collective-permute-start.1 = (f32[2,8,384]{2,1,0:T(8,128)S(1)}, f32[2,8,384]{2,1,0:T(8,128)S(1)}, u32[]{:S(2)}, u32[]{:S(2)}) collective-permute-start(f32[2,8,384]{2,1,0:T(8,128)S(1)} %get-tuple-element.265), channel_id=1, source_target_pairs={{1,0},{2,1},{3,2},{4,3},{5,4},{6,5},{7,6},{9,8},{10,9},{11,10},{12... | collective-permute-start | bytes 73736 | tf_op jit(solution)/shard_map/while/body/eval_jaxpr/ppermute | solution.py:17
  54.5 6.0 %copy-start = (f32[2,8,16,384]{3,2,0,1:T(8,128)}, f32[2,8,16,384]{3,2,0,1:T(8,128)S(1)}, u32[]{:S(2)}) copy-start(f32[2,8,16,384]{3,2,0,1:T(8,128)S(1)} %get-tuple-element.340) | copy-start | bytes 1179652 | tf_op jit(solution)/shard_map/while
  54.5 6.0 %collective-permute-start.2 = (f32[2,16,384]{2,1,0:T(8,128)S(1)}, f32[2,16,384]{2,1,0:T(8,128)S(1)}, u32[]{:S(2)}, u32[]{:S(2)}) collective-permute-start(f32[2,16,384]{2,1,0:T(8,128)S(1)} %get-tuple-element.314), channel_id=1, source_target_pairs={{0,8},{8,16},{16,24},{1,9},{9,17},{17,25},{2,10},{10,18},{18,26},{... | collective-permute-start | bytes 147464 | tf_op jit(solution)/shard_map/while/body/eval_jaxpr/ppermute | solution.py:27
  60.5 9.4 %collective-permute-start = (f32[2,8,384]{2,1,0:T(8,128)S(1)}, f32[2,8,384]{2,1,0:T(8,128)S(1)}, u32[]{:S(2)}, u32[]{:S(2)}) collective-permute-start(f32[2,8,384]{2,1,0:T(8,128)S(1)} %get-tuple-element.264), channel_id=1, source_target_pairs={{0,1},{1,2},{2,3},{3,4},{4,5},{5,6},{6,7},{8,9},{9,10},{10,11},{11... | collective-permute-start | bytes 73736 | tf_op jit(solution)/shard_map/while/body/eval_jaxpr/ppermute | solution.py:15
  62.4 7.5 %collective-permute-start.1 = (f32[2,8,384]{2,1,0:T(8,128)S(1)}, f32[2,8,384]{2,1,0:T(8,128)S(1)}, u32[]{:S(2)}, u32[]{:S(2)}) collective-permute-start(f32[2,8,384]{2,1,0:T(8,128)S(1)} %get-tuple-element.265), channel_id=1, source_target_pairs={{1,0},{2,1},{3,2},{4,3},{5,4},{6,5},{7,6},{9,8},{10,9},{11,10},{12... | collective-permute-start | bytes 73736 | tf_op jit(solution)/shard_map/while/body/eval_jaxpr/ppermute | solution.py:17
  79.8 6.0 %copy-start = (f32[2,8,16,384]{3,2,0,1:T(8,128)}, f32[2,8,16,384]{3,2,0,1:T(8,128)S(1)}, u32[]{:S(2)}) copy-start(f32[2,8,16,384]{3,2,0,1:T(8,128)S(1)} %get-tuple-element.340) | copy-start | bytes 1179652 | tf_op jit(solution)/shard_map/while
  79.8 6.0 %collective-permute-start.2 = (f32[2,16,384]{2,1,0:T(8,128)S(1)}, f32[2,16,384]{2,1,0:T(8,128)S(1)}, u32[]{:S(2)}, u32[]{:S(2)}) collective-permute-start(f32[2,16,384]{2,1,0:T(8,128)S(1)} %get-tuple-element.314), channel_id=1, source_target_pairs={{0,8},{8,16},{16,24},{1,9},{9,17},{17,25},{2,10},{10,18},{18,26},{... | collective-permute-start | bytes 147464 | tf_op jit(solution)/shard_map/while/body/eval_jaxpr/ppermute | solution.py:27
  85.8 9.4 %collective-permute-start = (f32[2,8,384]{2,1,0:T(8,128)S(1)}, f32[2,8,384]{2,1,0:T(8,128)S(1)}, u32[]{:S(2)}, u32[]{:S(2)}) collective-permute-start(f32[2,8,384]{2,1,0:T(8,128)S(1)} %get-tuple-element.264), channel_id=1, source_target_pairs={{0,1},{1,2},{2,3},{3,4},{4,5},{5,6},{6,7},{8,9},{9,10},{10,11},{11... | collective-permute-start | bytes 73736 | tf_op jit(solution)/shard_map/while/body/eval_jaxpr/ppermute | solution.py:15
  87.7 7.5 %collective-permute-start.1 = (f32[2,8,384]{2,1,0:T(8,128)S(1)}, f32[2,8,384]{2,1,0:T(8,128)S(1)}, u32[]{:S(2)}, u32[]{:S(2)}) collective-permute-start(f32[2,8,384]{2,1,0:T(8,128)S(1)} %get-tuple-element.265), channel_id=1, source_target_pairs={{1,0},{2,1},{3,2},{4,3},{5,4},{6,5},{7,6},{9,8},{10,9},{11,10},{12... | collective-permute-start | bytes 73736 | tf_op jit(solution)/shard_map/while/body/eval_jaxpr/ppermute | solution.py:17
  105.0 6.0 %copy-start = (f32[2,8,16,384]{3,2,0,1:T(8,128)}, f32[2,8,16,384]{3,2,0,1:T(8,128)S(1)}, u32[]{:S(2)}) copy-start(f32[2,8,16,384]{3,2,0,1:T(8,128)S(1)} %get-tuple-element.340) | copy-start | bytes 1179652 | tf_op jit(solution)/shard_map/while
  105.0 6.0 %collective-permute-start.2 = (f32[2,16,384]{2,1,0:T(8,128)S(1)}, f32[2,16,384]{2,1,0:T(8,128)S(1)}, u32[]{:S(2)}, u32[]{:S(2)}) collective-permute-start(f32[2,16,384]{2,1,0:T(8,128)S(1)} %get-tuple-element.314), channel_id=1, source_target_pairs={{0,8},{8,16},{16,24},{1,9},{9,17},{17,25},{2,10},{10,18},{18,26},{... | collective-permute-start | bytes 147464 | tf_op jit(solution)/shard_map/while/body/eval_jaxpr/ppermute | solution.py:27
  111.0 9.4 %collective-permute-start = (f32[2,8,384]{2,1,0:T(8,128)S(1)}, f32[2,8,384]{2,1,0:T(8,128)S(1)}, u32[]{:S(2)}, u32[]{:S(2)}) collective-permute-start(f32[2,8,384]{2,1,0:T(8,128)S(1)} %get-tuple-element.264), channel_id=1, source_target_pairs={{0,1},{1,2},{2,3},{3,4},{4,5},{5,6},{6,7},{8,9},{9,10},{10,11},{11... | collective-permute-start | bytes 73736 | tf_op jit(solution)/shard_map/while/body/eval_jaxpr/ppermute | solution.py:15
  113.0 7.5 %collective-permute-start.1 = (f32[2,8,384]{2,1,0:T(8,128)S(1)}, f32[2,8,384]{2,1,0:T(8,128)S(1)}, u32[]{:S(2)}, u32[]{:S(2)}) collective-permute-start(f32[2,8,384]{2,1,0:T(8,128)S(1)} %get-tuple-element.265), channel_id=1, source_target_pairs={{1,0},{2,1},{3,2},{4,3},{5,4},{6,5},{7,6},{9,8},{10,9},{11,10},{12... | collective-permute-start | bytes 73736 | tf_op jit(solution)/shard_map/while/body/eval_jaxpr/ppermute | solution.py:17
  130.3 6.0 %copy-start = (f32[2,8,16,384]{3,2,0,1:T(8,128)}, f32[2,8,16,384]{3,2,0,1:T(8,128)S(1)}, u32[]{:S(2)}) copy-start(f32[2,8,16,384]{3,2,0,1:T(8,128)S(1)} %get-tuple-element.340) | copy-start | bytes 1179652 | tf_op jit(solution)/shard_map/while
  130.3 6.0 %collective-permute-start.2 = (f32[2,16,384]{2,1,0:T(8,128)S(1)}, f32[2,16,384]{2,1,0:T(8,128)S(1)}, u32[]{:S(2)}, u32[]{:S(2)}) collective-permute-start(f32[2,16,384]{2,1,0:T(8,128)S(1)} %get-tuple-element.314), channel_id=1, source_target_pairs={{0,8},{8,16},{16,24},{1,9},{9,17},{17,25},{2,10},{10,18},{18,26},{... | collective-permute-start | bytes 147464 | tf_op jit(solution)/shard_map/while/body/eval_jaxpr/ppermute | solution.py:27
where the time goes:
time: 142 us; the launch traced here: 140 us
  starting transfers between devices  46.5 us (33%)
  other arithmetic  40.3 us (28%)
  local copies, waits for them, and re-layouts  26.9 us (19%)
  waiting for transfers between devices  24.2 us (17%)
    mul x24, other arithmetic, update_block(): scale_w[:, level]  29.8 us
    ppermute x5, starting transfers between devices, extended(): lax.ppermute(head, axis, [((i + 1) % count, i) for i in range(ends)])  23 us
    ppermute x4, starting transfers between devices, shifted(): return lax.ppermute(block, axis, route)  13.9 us
    ppermute x5, waiting for transfers between devices, extended(): lax.ppermute(tail, axis, [(i, (i + 1) % count) for i in range(ends)])  13.5 us
    ppermute x4, waiting for transfers between devices, shifted(): return lax.ppermute(block, axis, route)  9.95 us
    ppermute x5, starting transfers between devices, extended(): lax.ppermute(tail, axis, [(i, (i + 1) % count) for i in range(ends)])  9.58 us
    while x7, local copies, waits for them, and re-layouts, shards(): _, adjoint = lax.fori_loop(0, lax.axis_size('sweep'), advance, start)  6.33 us
    mul x4, other arithmetic, update_block(): slow_w[level] * previous  4.97 us
  transfers between devices with their start and end apart: 14, of which 6 were waited for; matrix products, arithmetic and copies ran while one was open for 8% of the time, Pallas kernels for 0%

commit v1 on v0

v1 whole, which is shorter than its diff:
```python
import functools

import jax
import jax.numpy as jnp
from jax import lax
from jax.experimental import pallas as pl
from jax.experimental.pallas import tpu as pltpu
from jax.sharding import PartitionSpec as P

MESH = pl.DeviceIdType.MESH
HALO = 8


def kernel(
    n_sweep, n_lat,
    t_ref, r_ref, s_ref, a_ref, topo_ref,
    adj_ref, grad_ref,
    T, R, S, A, TP, C, IN,
    local_sem, halo_send, halo_recv, topo_send, topo_recv, flow_send, flow_recv,
):
    sources, planes, cols, ny = t_ref.shape
    rows = cols + 2 * HALO
    own = pl.ds(HALO, cols)
    sweep = lax.axis_index("sweep")
    lat = lax.axis_index("lat")
    has_left = lat > 0
    has_right = lat < n_lat - 1
    has_up = sweep > 0
    has_down = sweep < n_sweep - 1

    local = [
        pltpu.make_async_copy(t_ref, T.at[:, :, own], local_sem.at[0]),
        pltpu.make_async_copy(s_ref, S.at[:, own], local_sem.at[1]),
        pltpu.make_async_copy(a_ref, A.at[:, own], local_sem.at[2]),
        pltpu.make_async_copy(topo_ref, TP.at[own], local_sem.at[3]),
        pltpu.make_async_copy(r_ref, R.at[:, :, own], local_sem.at[4]),
    ]
    for copy in local:
        copy.start()

    barrier = pltpu.get_barrier_semaphore()
    near = [
        (has_left, sweep, lat - 1),
        (has_right, sweep, lat + 1),
    ]
    for step, ok in ((-1, has_up), (1, has_down)):
        near += [
            (ok, sweep + step, lat),
            (ok & has_left, sweep + step, lat - 1),
            (ok & has_right, sweep + step, lat + 1),
        ]
    for ok, z, x in near:
        @pl.when(ok)
        def _():
            pl.semaphore_signal(barrier, inc=1, device_id=(z, x), device_id_type=MESH)
    peers = sum(ok.astype(jnp.int32) for ok, _, _ in near)
    pl.semaphore_wait(barrier, peers)

    def halo_copies(side, level):
        src = pl.ds(0, HALO) if side == 0 else pl.ds(cols - HALO, HALO)
        dst = pl.ds(HALO + cols, HALO) if side == 0 else pl.ds(0, HALO)
        peer = (sweep, lat - 1) if side == 0 else (sweep, lat + 1)
        pairs = [
            (t_ref.at[:, level, src], T.at[:, level, dst]),
            (s_ref.at[level, src], S.at[level, dst]),
            (a_ref.at[level, src], A.at[level, dst]),
            (r_ref.at[:, level, src], R.at[:, level, dst]),
        ]
        return [
            pltpu.make_async_remote_copy(
                src_ref=x, dst_ref=y,
                send_sem=halo_send.at[side, level, i], recv_sem=halo_recv.at[side, level, i],
                device_id=peer, device_id_type=MESH,
            )
            for i, (x, y) in enumerate(pairs)
        ]

    def topo_copy(side):
        src = pl.ds(0, HALO) if side == 0 else pl.ds(cols - HALO, HALO)
        dst = pl.ds(HALO + cols, HALO) if side == 0 else pl.ds(0, HALO)
        peer = (sweep, lat - 1) if side == 0 else (sweep, lat + 1)
        return pltpu.make_async_remote_copy(
            src_ref=topo_ref.at[src], dst_ref=TP.at[dst],
            send_sem=topo_send.at[side], recv_sem=topo_recv.at[side],
            device_id=peer, device_id_type=MESH,
        )

    sides = ((0, has_left), (1, has_right))
    for side, ok in sides:
        @pl.when(ok)
        def _():
            topo_copy(side).start()

    def send_level(level, carry):
        for side, ok in sides:
            @pl.when(ok)
            def _():
                for copy in halo_copies(side, level):
                    copy.start()
        return carry

    lax.fori_loop(0, planes, send_level, 0)

    for ok, dst in ((has_left, pl.ds(0, HALO)), (has_right, pl.ds(HALO + cols, HALO))):
        @pl.when(jnp.logical_not(ok))
        def _():
            T[:, :, dst] = jnp.zeros((sources, planes, HALO, ny), jnp.float32)
            R[:, :, dst] = jnp.zeros((sources, planes, HALO, ny), jnp.float32)
            S[:, dst] = jnp.zeros((planes, HALO, ny), jnp.float32)
            A[:, dst] = jnp.zeros((planes, HALO, ny), jnp.float32)
            TP[dst] = jnp.full((HALO, ny), n_sweep * planes, jnp.int32)
            IN[:, dst] = jnp.zeros((sources, HALO, ny), jnp.float32)

    @pl.when(jnp.logical_not(has_up))
    def _():
        IN[...] = jnp.zeros((sources, rows, ny), jnp.float32)

    for copy in local:
        copy.wait()
    arrivals = ((0, has_right), (1, has_left))
    for side, ok in arrivals:
        @pl.when(ok)
        def _():
            topo_copy(side).wait_recv()

    lane = lax.broadcasted_iota(jnp.int32, (rows, ny), 1)
    first = lane == 0
    last = lane == ny - 1

    def log_part(d):
        return jnp.log(1.0 + jnp.exp(-jnp.abs(d)))

    def weigh(level, carry):
        for side, ok in arrivals:
            @pl.when(ok)
            def _():
                for copy in halo_copies(side, level):
                    copy.wait_recv()
        slow = S[level]
        base = slow + A[level]
        active = sweep * planes + level >= TP[...]
        for k in range(sources):
            t = T[k, level]
            d = t - pltpu.roll(t, 1, 0)
            p = log_part(d)
            west = jnp.maximum(d, 0.0) + p
            east = pltpu.roll(jnp.maximum(-d, 0.0) + p, rows - 1, 0)
            d = t - jnp.where(first, 0.0, pltpu.roll(t, 1, 1))
            p = log_part(d)
            north = jnp.maximum(d, 0.0) + p
            end = jnp.maximum(t, 0.0) + log_part(t)
            south = jnp.where(last, end, pltpu.roll(jnp.maximum(-d, 0.0) + p, ny - 1, 1))
            scale = jnp.where(active, 1.0 / (base + west + east + north + south), 0.0)
            C[k, level, 0] = scale * R[k, level]
            C[k, level, 1] = scale * slow
            C[k, level, 2] = scale * west
            C[k, level, 3] = scale * east
            C[k, level, 4] = jnp.where(first, 0.0, scale * north)
            C[k, level, 5] = jnp.where(last, 0.0, scale * south)
        return carry

    lax.fori_loop(0, planes, weigh, 0)

    def flow_copies(k):
        low, high = pl.ds(0, HALO), pl.ds(HALO + cols, HALO)
        parts = [
            (pl.ds(0, cols), own, lat),
            (pl.ds(0, HALO), high, lat - 1),
            (pl.ds(cols - HALO, HALO), low, lat + 1),
        ]
        return [
            pltpu.make_async_remote_copy(
                src_ref=adj_ref.at[k, planes - 1, src], dst_ref=IN.at[k, dst],
                send_sem=flow_send.at[k, i], recv_sem=flow_recv.at[k, i],
                device_id=(sweep + 1, x), device_id_type=MESH,
            )
            for i, (src, dst, x) in enumerate(parts)
        ]

    for k in range(sources):
        copies = flow_copies(k)
        for copy, ok in zip(copies, (has_up, has_up & has_right, has_up & has_left)):
            @pl.when(ok)
            def _():
                copy.wait_recv()

        def advance(level, previous):
            current = (
                C[k, level, 0]
                + C[k, level, 1] * previous
                + C[k, level, 2] * pltpu.roll(previous, 1, 0)
                + C[k, level, 3] * pltpu.roll(previous, rows - 1, 0)
                + C[k, level, 4] * pltpu.roll(previous, 1, 1)
                + C[k, level, 5] * pltpu.roll(previous, ny - 1, 1)
            )
            adj_ref[k, level] = current[HALO : HALO + cols]
            return current

        lax.fori_loop(0, planes, advance, IN[k])
        for copy, ok in zip(copies, (has_down, has_down & has_left, has_down & has_right)):
            @pl.when(ok)
            def _():
                copy.start()

    def total(level, carry):
        field = adj_ref[0, level]
        for k in range(1, sources):
            field = field + adj_ref[k, level]
        grad_ref[level] = S[level, own] * field
        return carry

    lax.fori_loop(0, planes, total, 0)

    def drain(level, carry):
        for side, ok in sides:
            @pl.when(ok)
            def _():
                for copy in halo_copies(side, level):
                    copy.wait_send()
        return carry

    lax.fori_loop(0, planes, drain, 0)
    for side, ok in sides:
        @pl.when(ok)
        def _():
            topo_copy(side).wait_send()
    for k in range(sources):
        for copy, ok in zip(flow_copies(k), (has_down, has_down & has_left, has_down & has_right)):
            @pl.when(ok)
            def _():
                copy.wait_send()


def shards(n_sweep, n_lat, traveltime, residual, slowness, attenuation, topography):
    sources, planes, cols, ny = traveltime.shape
    rows = cols + 2 * HALO
    f32 = jnp.float32
    return pl.pallas_call(
        functools.partial(kernel, n_sweep, n_lat),
        out_shape=(
            jax.ShapeDtypeStruct(traveltime.shape, f32),
            jax.ShapeDtypeStruct(slowness.shape, f32),
        ),
        in_specs=[pl.BlockSpec(memory_space=pl.ANY)] * 5,
        out_specs=(pl.BlockSpec(memory_space=pltpu.VMEM),) * 2,
        scratch_shapes=[
            pltpu.VMEM((sources, planes, rows, ny), f32),
            pltpu.VMEM((sources, planes, rows, ny), f32),
            pltpu.VMEM((planes, rows, ny), f32),
            pltpu.VMEM((planes, rows, ny), f32),
            pltpu.VMEM((rows, ny), jnp.int32),
            pltpu.VMEM((sources, planes, 6, rows, ny), f32),
            pltpu.VMEM((sources, rows, ny), f32),
            pltpu.SemaphoreType.DMA((5,)),
            pltpu.SemaphoreType.DMA((2, planes, 4)),
            pltpu.SemaphoreType.DMA((2, planes, 4)),
            pltpu.SemaphoreType.DMA((2,)),
            pltpu.SemaphoreType.DMA((2,)),
            pltpu.SemaphoreType.DMA((sources, 3)),
            pltpu.SemaphoreType.DMA((sources, 3)),
        ],
        compiler_params=pltpu.CompilerParams(
            collective_id=0, has_side_effects=True, vmem_limit_bytes=60 * 1024 * 1024
        ),
    )(traveltime, residual, slowness, attenuation, topography)


def solution(mesh):
    in_specs = (
        P(None, "sweep", "lat", None),
        P(None, "sweep", "lat", None),
        P("sweep", "lat", None),
        P("sweep", "lat", None),
        P("lat", None),
    )
    out_specs = (P(None, "sweep", "lat", None), P("sweep", "lat", None))
    body = functools.partial(shards, mesh.shape["sweep"], mesh.shape["lat"])
    return jax.shard_map(body, mesh=mesh, in_specs=in_specs, out_specs=out_specs, check_vma=False)
```

time: 142 us -> 37.1 us (0.26)
  the two profiles are of different devices: /device:TPU:12 before, /device:TPU:27 now
where the time goes in v1:
time: 37.1 us; the launch traced here: 37 us
  Pallas kernels  33.8 us (91%)
  local copies, waits for them, and re-layouts  2.49 us (7%)
  between operations  0.65 us (2%)
    pallas_call x1, Pallas kernels, shards(): pl.pallas_call(functools.partial(kernel, n_sweep, n_lat), out_shape=(jax....  33.8 us
    unnamed x4, local copies, waits for them, and re-layouts  2.49 us

profile of v1, /device:TPU:27, one launch (start us, length us, event | category | flops | bytes accessed | tf_op | source)
XLA Modules:
  0.0 37.0 jit_solution(126532833000303629)
XLA Ops:
  0.6 33.8 %shard_map.68 = (f32[2,8,16,384]{3,2,1,0:T(8,128)}, f32[8,16,384]{2,1,0:T(8,128)}) custom-call(f32[2,8,16,384]{3,2,1,0:T(8,128)} %t_ref.1, f32[2,8,16,384]{3,2,1,0:T(8,128)} %r_ref.1, f32[8,16,384]{2,1,0:T(8,128)} %s_ref.1, f32[8,16,384]{2,1,0:T(8,128)} %a_ref.1, s32[16,384]{1,0:T(8,128)} %topo_ref.1), custom_call_target="tpu_custom_call" | custom-call | tf_op jit(solution)/shard_map/pallas_call | solution.py:238
  34.5 0.0 copy-start
  34.5 1.8 %copy.9 = f32[2,8,16,384]{3,2,1,0:T(8,128)} copy(f32[2,8,16,384]{3,2,1,0:T(8,128)} %get-tuple-element.4) | data formatting | bytes 786432
  36.3 0.0 copy-done
  36.3 0.7 %copy.10 = f32[8,16,384]{2,1,0:T(8,128)} copy(f32[8,16,384]{2,1,0:T(8,128)S(1)} %copy-done) | data formatting | bytes 393216
Async XLA Ops:
  34.5 1.8 %copy-start = (f32[8,16,384]{2,1,0:T(8,128)S(1)}, f32[8,16,384]{2,1,0:T(8,128)}, u32[]{:S(2)}) copy-start(f32[8,16,384]{2,1,0:T(8,128)} %get-tuple-element.5) | copy-start | bytes 589828

commit v2 on v1

--- a/solution.py
+++ b/solution.py
@@ -57,15 +57,22 @@
     pl.semaphore_wait(barrier, peers)
 
     def halo_copies(side, level):
-        src = pl.ds(0, HALO) if side == 0 else pl.ds(cols - HALO, HALO)
-        dst = pl.ds(HALO + cols, HALO) if side == 0 else pl.ds(0, HALO)
         peer = (sweep, lat - 1) if side == 0 else (sweep, lat + 1)
-        pairs = [
-            (t_ref.at[:, level, src], T.at[:, level, dst]),
-            (s_ref.at[level, src], S.at[level, dst]),
-            (a_ref.at[level, src], A.at[level, dst]),
-            (r_ref.at[:, level, src], R.at[:, level, dst]),
-        ]
+
+        def ends(n):
+            if side == 0:
+                return pl.ds(0, n), pl.ds(HALO + cols, n)
+            return pl.ds(cols - n, n), pl.ds(HALO - n, n)
+
+        src, dst = ends(HALO - level)
+        pairs = [(t_ref.at[:, level, src], T.at[:, level, dst])]
+        if level < planes - 1:
+            src, dst = ends(HALO - 1 - level)
+            pairs += [
+                (s_ref.at[level, src], S.at[level, dst]),
+                (a_ref.at[level, src], A.at[level, dst]),
+                (r_ref.at[:, level, src], R.at[:, level, dst]),
+            ]
         return [
             pltpu.make_async_remote_copy(
                 src_ref=x, dst_ref=y,
@@ -99,7 +106,8 @@
                     copy.start()
         return carry
 
-    lax.fori_loop(0, planes, send_level, 0)
+    for level in range(planes):
+        send_level(level, 0)
 
     for ok, dst in ((has_left, pl.ds(0, HALO)), (has_right, pl.ds(HALO + cols, HALO))):
         @pl.when(jnp.logical_not(ok))
@@ -159,7 +167,8 @@
             C[k, level, 5] = jnp.where(last, 0.0, scale * south)
         return carry
 
-    lax.fori_loop(0, planes, weigh, 0)
+    for level in range(planes):
+        weigh(level, 0)
 
     def flow_copies(k):
         low, high = pl.ds(0, HALO), pl.ds(HALO + cols, HALO)
@@ -219,7 +228,8 @@
                     copy.wait_send()
         return carry
 
-    lax.fori_loop(0, planes, drain, 0)
+    for level in range(planes):
+        drain(level, 0)
     for side, ok in sides:
         @pl.when(ok)
         def _():
@@ -260,9 +270,9 @@
             pltpu.SemaphoreType.DMA((sources, 3)),
         ],
         compiler_params=pltpu.CompilerParams(
-            collective_id=0, has_side_effects=True, vmem_limit_bytes=60 * 1024 * 1024
+            collective_id=0, has_side_effects=True, vmem_limit_bytes=24 * 1024 * 1024
         ),
-    )(traveltime, residual, slowness, attenuation, topography)
+    )(*[pltpu.with_memory_space_constraint(x, pltpu.HBM) for x in (traveltime, residual, slowness, attenuation, topography)])
 
 
 def solution(mesh):

time: 37.1 us -> 28.8 us (0.78)
  Pallas kernels: 33.8 us -> 26.6 us
  local copies, waits for them, and re-layouts: 2.49 us -> 1.42 us
    pallas_call x1, Pallas kernels: 33.8 us -> 26.6 us  [shards(): pl.pallas_call(functools.partial(kernel, n_sweep, n_lat), out_shape=(jax....]
    unnamed x4 -> x2, local copies, waits for them, and re-layouts: 2.49 us -> 1.42 us
where the time goes in v2:
time: 28.8 us; the launch traced here: 28.6 us
  Pallas kernels  26.6 us (92%)
  local copies, waits for them, and re-layouts  1.42 us (5%)
  between operations  0.64 us (2%)
    pallas_call x1, Pallas kernels, shards(): pl.pallas_call(functools.partial(kernel, n_sweep, n_lat), out_shape=(jax....  26.6 us
    unnamed x2, local copies, waits for them, and re-layouts  1.42 us

profile of v2, /device:TPU:27, one launch (start us, length us, event | category | flops | bytes accessed | tf_op | source)
XLA Modules:
  0.0 28.6 jit_solution(4113807991032252875)
XLA Ops:
  0.6 26.6 %shard_map.68 = (f32[2,8,16,384]{3,2,1,0:T(8,128)S(1)}, f32[8,16,384]{2,1,0:T(8,128)S(1)}) custom-call(f32[2,8,16,384]{3,2,1,0:T(8,128)} %t_ref.1, f32[2,8,16,384]{3,2,1,0:T(8,128)} %r_ref.1, f32[8,16,384]{2,1,0:T(8,128)} %s_ref.1, f32[8,16,384]{2,1,0:T(8,128)} %a_ref.1, s32[16,384]{1,0:T(8,128)} %topo_ref.1), custom_call_target="tpu_custom_call" | custom-call | tf_op jit(solution)/shard_map/pallas_call | solution.py:248
  27.2 0.7 %copy.9 = f32[2,8,16,384]{3,2,1,0:T(8,128)} copy(f32[2,8,16,384]{3,2,1,0:T(8,128)S(1)} %get-tuple-element.4) | data formatting | bytes 786432
  28.0 0.7 %copy.10 = f32[8,16,384]{2,1,0:T(8,128)} copy(f32[8,16,384]{2,1,0:T(8,128)S(1)} %get-tuple-element.5) | data formatting | bytes 393216

commit v3 on v2

--- a/solution.py
+++ b/solution.py
@@ -16,7 +16,7 @@
     t_ref, r_ref, s_ref, a_ref, topo_ref,
     adj_ref, grad_ref,
     T, R, S, A, TP, C, IN,
-    local_sem, halo_send, halo_recv, topo_send, topo_recv, flow_send, flow_recv,
+    local_sem, halo_send, halo_recv, topo_send, topo_recv, mid_send, mid_recv, flow_send, flow_recv,
 ):
     sources, planes, cols, ny = t_ref.shape
     rows = cols + 2 * HALO
@@ -37,6 +37,15 @@
     ]
     for copy in local:
         copy.start()
+
+    for ok, dst in ((has_left, pl.ds(0, HALO)), (has_right, pl.ds(HALO + cols, HALO))):
+        @pl.when(jnp.logical_not(ok))
+        def _():
+            IN[:, dst] = jnp.zeros((sources, HALO, ny), jnp.float32)
+
+    @pl.when(jnp.logical_not(has_up))
+    def _():
+        IN[...] = jnp.zeros((sources, rows, ny), jnp.float32)
 
     barrier = pltpu.get_barrier_semaphore()
     near = [
@@ -56,7 +65,7 @@
     peers = sum(ok.astype(jnp.int32) for ok, _, _ in near)
     pl.semaphore_wait(barrier, peers)
 
-    def halo_copies(side, level):
+    def halo_copies(side, level, depth):
         peer = (sweep, lat - 1) if side == 0 else (sweep, lat + 1)
 
         def ends(n):
@@ -64,10 +73,10 @@
                 return pl.ds(0, n), pl.ds(HALO + cols, n)
             return pl.ds(cols - n, n), pl.ds(HALO - n, n)
 
-        src, dst = ends(HALO - level)
+        src, dst = ends(depth - level)
         pairs = [(t_ref.at[:, level, src], T.at[:, level, dst])]
-        if level < planes - 1:
-            src, dst = ends(HALO - 1 - level)
+        if level < depth - 1:
+            src, dst = ends(depth - 1 - level)
             pairs += [
                 (s_ref.at[level, src], S.at[level, dst]),
                 (a_ref.at[level, src], A.at[level, dst]),
@@ -82,6 +91,20 @@
             for i, (x, y) in enumerate(pairs)
         ]
 
+    half = planes // 2
+
+    def each_halo(tests, level, act):
+        for side, ok in tests:
+            if level >= half:
+                cases = ((ok, planes),)
+            else:
+                cases = ((ok & has_up, planes), (ok & jnp.logical_not(has_up), half))
+            for case, depth in cases:
+                @pl.when(case)
+                def _():
+                    for copy in halo_copies(side, level, depth):
+                        act(copy)
+
     def topo_copy(side):
         src = pl.ds(0, HALO) if side == 0 else pl.ds(cols - HALO, HALO)
         dst = pl.ds(HALO + cols, HALO) if side == 0 else pl.ds(0, HALO)
@@ -98,16 +121,8 @@
         def _():
             topo_copy(side).start()
 
-    def send_level(level, carry):
-        for side, ok in sides:
-            @pl.when(ok)
-            def _():
-                for copy in halo_copies(side, level):
-                    copy.start()
-        return carry
-
     for level in range(planes):
-        send_level(level, 0)
+        each_halo(sides, level, lambda copy: copy.start())
 
     for ok, dst in ((has_left, pl.ds(0, HALO)), (has_right, pl.ds(HALO + cols, HALO))):
         @pl.when(jnp.logical_not(ok))
@@ -117,11 +132,6 @@
             S[:, dst] = jnp.zeros((planes, HALO, ny), jnp.float32)
             A[:, dst] = jnp.zeros((planes, HALO, ny), jnp.float32)
             TP[dst] = jnp.full((HALO, ny), n_sweep * planes, jnp.int32)
-            IN[:, dst] = jnp.zeros((sources, HALO, ny), jnp.float32)
-
-    @pl.when(jnp.logical_not(has_up))
-    def _():
-        IN[...] = jnp.zeros((sources, rows, ny), jnp.float32)
 
     for copy in local:
         copy.wait()
@@ -138,12 +148,8 @@
     def log_part(d):
         return jnp.log(1.0 + jnp.exp(-jnp.abs(d)))
 
-    def weigh(level, carry):
-        for side, ok in arrivals:
-            @pl.when(ok)
-            def _():
-                for copy in halo_copies(side, level):
-                    copy.wait_recv()
+    def weigh(level):
+        each_halo(arrivals, level, lambda copy: copy.wait_recv())
         slow = S[level]
         base = slow + A[level]
         active = sweep * planes + level >= TP[...]
@@ -165,10 +171,49 @@
             C[k, level, 3] = scale * east
             C[k, level, 4] = jnp.where(first, 0.0, scale * north)
             C[k, level, 5] = jnp.where(last, 0.0, scale * south)
-        return carry
-
-    for level in range(planes):
-        weigh(level, 0)
+
+    def stepper(k):
+        def advance(level, previous):
+            current = (
+                C[k, level, 0]
+                + C[k, level, 1] * previous
+                + C[k, level, 2] * pltpu.roll(previous, 1, 0)
+                + C[k, level, 3] * pltpu.roll(previous, rows - 1, 0)
+                + C[k, level, 4] * pltpu.roll(previous, 1, 1)
+                + C[k, level, 5] * pltpu.roll(previous, ny - 1, 1)
+            )
+            adj_ref[k, level] = current[HALO : HALO + cols]
+            return current
+
+        return advance
+
+    def mid_copy(k, side):
+        if side == 0:
+            src, dst, x = pl.ds(0, half), pl.ds(HALO + cols, half), lat - 1
+        else:
+            src, dst, x = pl.ds(cols - half, half), pl.ds(HALO - half, half), lat + 1
+        return pltpu.make_async_remote_copy(
+            src_ref=adj_ref.at[k, half - 1, src], dst_ref=IN.at[k, dst],
+            send_sem=mid_send.at[k, side], recv_sem=mid_recv.at[k, side],
+            device_id=(sweep, x), device_id_type=MESH,
+        )
+
+    for level in range(half):
+        weigh(level)
+
+    @pl.when(jnp.logical_not(has_up))
+    def _():
+        for k in range(sources):
+            zero = jnp.zeros((rows, ny), jnp.float32)
+            current = lax.fori_loop(0, half, stepper(k), zero)
+            for side, ok in sides:
+                @pl.when(ok)
+                def _():
+                    mid_copy(k, side).start()
+            IN[k, own] = current[HALO : HALO + cols]
+
+    for level in range(half, planes):
+        weigh(level)
 
     def flow_copies(k):
         low, high = pl.ds(0, HALO), pl.ds(HALO + cols, HALO)
@@ -193,19 +238,12 @@
             def _():
                 copy.wait_recv()
 
-        def advance(level, previous):
-            current = (
-                C[k, level, 0]
-                + C[k, level, 1] * previous
-                + C[k, level, 2] * pltpu.roll(previous, 1, 0)
-                + C[k, level, 3] * pltpu.roll(previous, rows - 1, 0)
-                + C[k, level, 4] * pltpu.roll(previous, 1, 1)
-                + C[k, level, 5] * pltpu.roll(previous, ny - 1, 1)
-            )
-            adj_ref[k, level] = current[HALO : HALO + cols]
-            return current
-
-        lax.fori_loop(0, planes, advance, IN[k])
+        for side, ok in arrivals:
+            @pl.when(ok & jnp.logical_not(has_up))
+            def _():
+                mid_copy(k, side).wait_recv()
+
+        lax.fori_loop(jnp.where(has_up, 0, half), planes, stepper(k), IN[k])
         for copy, ok in zip(copies, (has_down, has_down & has_left, has_down & has_right)):
             @pl.when(ok)
             def _():
@@ -220,16 +258,13 @@
 
     lax.fori_loop(0, planes, total, 0)
 
-    def drain(level, carry):
+    for level in range(planes):
+        each_halo(sides, level, lambda copy: copy.wait_send())
+    for k in range(sources):
         for side, ok in sides:
-            @pl.when(ok)
-            def _():
-                for copy in halo_copies(side, level):
-                    copy.wait_send()
-        return carry
-
-    for level in range(planes):
-        drain(level, 0)
+            @pl.when(ok & jnp.logical_not(has_up))
+            def _():
+                mid_copy(k, side).wait_send()
     for side, ok in sides:
         @pl.when(ok)
         def _():
@@ -266,6 +301,8 @@
             pltpu.SemaphoreType.DMA((2, planes, 4)),
             pltpu.SemaphoreType.DMA((2,)),
             pltpu.SemaphoreType.DMA((2,)),
+            pltpu.SemaphoreType.DMA((sources, 2)),
+            pltpu.SemaphoreType.DMA((sources, 2)),
             pltpu.SemaphoreType.DMA((sources, 3)),
             pltpu.SemaphoreType.DMA((sources, 3)),
         ],

time: 28.8 us -> 27.2 us (0.944)
  Pallas kernels: 26.6 us -> 25 us
    pallas_call x1, Pallas kernels: 26.6 us -> 25 us  [shards(): pl.pallas_call(functools.partial(kernel, n_sweep, n_lat), out_shape=(jax....]
where the time goes in v3:
time: 27.2 us; the launch traced here: 27 us
  Pallas kernels  25 us (92%)
  local copies, waits for them, and re-layouts  1.42 us (5%)
  between operations  0.64 us (2%)
    pallas_call x1, Pallas kernels, shards(): pl.pallas_call(functools.partial(kernel, n_sweep, n_lat), out_shape=(jax....  25 us
    unnamed x2, local copies, waits for them, and re-layouts  1.42 us

profile of v3, /device:TPU:27, one launch (start us, length us, event | category | flops | bytes accessed | tf_op | source)
XLA Modules:
  0.0 27.0 jit_solution(16386219179510829053)
XLA Ops:
  0.6 25.0 %shard_map.68 = (f32[2,8,16,384]{3,2,1,0:T(8,128)S(1)}, f32[8,16,384]{2,1,0:T(8,128)S(1)}) custom-call(f32[2,8,16,384]{3,2,1,0:T(8,128)} %t_ref.1, f32[2,8,16,384]{3,2,1,0:T(8,128)} %r_ref.1, f32[8,16,384]{2,1,0:T(8,128)} %s_ref.1, f32[8,16,384]{2,1,0:T(8,128)} %a_ref.1, s32[16,384]{1,0:T(8,128)} %topo_ref.1), custom_call_target="tpu_custom_call" | custom-call | tf_op jit(solution)/shard_map/pallas_call | solution.py:283
  25.6 0.7 %copy.9 = f32[2,8,16,384]{3,2,1,0:T(8,128)} copy(f32[2,8,16,384]{3,2,1,0:T(8,128)S(1)} %get-tuple-element.4) | data formatting | bytes 786432
  26.4 0.7 %copy.10 = f32[8,16,384]{2,1,0:T(8,128)} copy(f32[8,16,384]{2,1,0:T(8,128)S(1)} %get-tuple-element.5) | data formatting | bytes 393216
